TPU v7x, 512 devices: a whole 4x4x16 slice. The times are simulated.
512 devices in a mesh: wave: 128 (over z, y, core), lev: 4 (over x).
Axes of the slice: x: 4, y: 4, z: 16, core: 2. Of those that a mesh axis runs over, the one named last changes fastest.
Arguments:
- coeffs: bfloat16 [768, 2, 4, 16, 768], P('wave', None, None, 'lev'), may hold values from -6 to 6
- legendre: bfloat16 [768, 768, 384], P('wave'), may hold values from -6 to 6
- slot_wave: int32 [768], replicated, may hold values from 0 to 767, as said below
- lon_points: int32 [768], replicated, may hold values from 20 to 3088, as said below
- quad_weights: float32 [768], replicated, may hold values from 0.5 to 1.5
Outputs:
- spectral_out: bfloat16 [768, 2, 4, 16, 768], P('wave', None, None, 'lev')
Inputs may be any that keep to these rules, and one draw needn't show every extreme that they name: `slot_wave`: a permutation of the wavenumbers in which slots 2q and 2q+1 hold wavenumbers m and 767-m, so the 6 slots of one device are whole pairs. `lon_points`: every value is 4 i + 16 for a whole number i; values rise from latitude 0 to latitude 384 - 1, and lon_points[767-j] equals lon_points[j].
All inputs are finite; a program needn't handle non-finite values.
Results may differ from a plain program's by a relative error of at most 0.0075.
Values may be sent and summed in bfloat16 or wider, within the bound.
A program may use at most 64 MiB of HBM per device.

v0:
```python
import math

import jax
import jax.numpy as jnp
from jax import lax
from jax.sharding import PartitionSpec as P

TWO_PI = 2.0 * math.pi
block_width = 512
highest = lax.Precision.HIGHEST


def prefix(array, axis, combine, identity):
    peers, place = (lax.axis_size(axis), lax.axis_index(axis))
    everything = lax.all_gather(array.astype(jnp.bfloat16), axis)
    start = jnp.broadcast_to(jnp.asarray(identity, array.dtype), array.shape)

    def lap(k, before):
        reached = k < place
        new = combine(before, everything[k].astype(array.dtype))
        return jnp.where(reached, new, before)

    return lax.fori_loop(0, peers, lap, start)


def angle_pair(first_factor, second_factor, points):
    phases = first_factor[:, None] * second_factor[None, :] % points
    angles = phases.astype(jnp.float32) * (TWO_PI / points.astype(jnp.float32))
    return (jnp.cos(angles), jnp.sin(angles))


def transform_tables(wave_numbers, points, blocks):
    starts = jnp.arange(blocks, dtype=jnp.int32) * block_width
    twist_cos, twist_sin = angle_pair(starts, wave_numbers, points)
    base_cos, base_sin = angle_pair(wave_numbers, jnp.arange(block_width, dtype=jnp.int32), points)
    base_table = jnp.concatenate([base_cos, -base_sin], axis=0)
    return (twist_cos, twist_sin, base_table)


def to_grid(fourier, tables, points, wave_numbers):
    twist_cos, twist_sin, base_table = tables
    blocks = twist_cos.shape[0]
    wave_total = fourier.shape[2]
    half_count = fourier.shape[1] // 2
    top_wave = jnp.minimum(wave_total - 1, (points - 1) // 2)
    factor = jnp.where(wave_numbers == 0, 1.0, 2.0).astype(jnp.float32)
    factor = factor * (wave_numbers <= top_wave).astype(jnp.float32) / math.sqrt(wave_total)
    real_part = (fourier[:, :half_count] * factor)[:, None]
    imag_part = (fourier[:, half_count:] * factor)[:, None]
    turn_cos = twist_cos[None, :, None, :]
    turn_sin = twist_sin[None, :, None, :]
    turned_real = real_part * turn_cos - imag_part * turn_sin
    turned_imag = real_part * turn_sin + imag_part * turn_cos
    stacked = jnp.concatenate([turned_real, turned_imag], axis=3)
    grid_field = jnp.einsum("lbcs,sq->lcbq", stacked, base_table, precision=highest)
    grid_field = grid_field.reshape(fourier.shape[0], half_count, blocks * block_width)
    inside = (jnp.arange(blocks * block_width, dtype=jnp.int32) < points).astype(jnp.float32)
    return grid_field * inside


def to_spectral(forcing, tables, points, wave_numbers):
    twist_cos, twist_sin, base_table = tables
    blocks = twist_cos.shape[0]
    wave_total = wave_numbers.shape[0]
    shaped = forcing.reshape(forcing.shape[0], forcing.shape[1], blocks, block_width)
    partial_value = jnp.einsum("lcbq,sq->lbcs", shaped, base_table, precision=highest)
    part_real = partial_value[..., :wave_total]
    part_imag = partial_value[..., wave_total:]
    turn_cos = twist_cos[None, :, None, :]
    turn_sin = twist_sin[None, :, None, :]
    real_out = jnp.sum(turn_cos * part_real + turn_sin * part_imag, axis=1)
    imag_out = jnp.sum(turn_cos * part_imag - turn_sin * part_real, axis=1)
    top_wave = jnp.minimum(wave_total - 1, (points - 1) // 2)
    out_scale = (
        (wave_numbers <= top_wave).astype(jnp.float32)
        * math.sqrt(wave_total)
        / points.astype(jnp.float32)
    )
    return jnp.concatenate([real_out, imag_out], axis=1) * out_scale


def degree_masks(waves_local, wave_total):
    degree = jnp.arange(wave_total, dtype=jnp.int32)
    keep_mask = degree[None, :] >= waves_local[:, None]
    flipped = jnp.where((degree[None, :] + waves_local[:, None]) % 2 == 0, 1.0, -1.0)
    return (keep_mask, flipped)


def padded_inverse(spectral, legendre, waves_local):
    wave_total = spectral.shape[2]
    keep_mask, flipped = degree_masks(waves_local, wave_total)
    kept_spec = jnp.where(keep_mask[:, None, :], spectral, jnp.zeros_like(spectral))
    signed = kept_spec * flipped[:, None, :].astype(jnp.bfloat16)
    north_part = jnp.einsum("scn,snj->cjs", kept_spec, legendre, preferred_element_type=jnp.float32)
    south_part = jnp.einsum("scn,snj->cjs", signed, legendre, preferred_element_type=jnp.float32)
    return (north_part / math.sqrt(wave_total), south_part / math.sqrt(wave_total))


def padded_direct(north_grid, south_grid, legendre, waves_local, lat_total):
    keep_mask, flipped = degree_masks(waves_local, legendre.shape[1])
    north_part = jnp.einsum(
        "snj,cjs->scn", legendre, north_grid, preferred_element_type=jnp.float32
    )
    south_part = jnp.einsum(
        "snj,cjs->scn", legendre, south_grid, preferred_element_type=jnp.float32
    )
    total = (north_part + flipped[:, None, :] * south_part) * keep_mask[:, None, :].astype(
        jnp.float32
    )
    return (total / math.sqrt(lat_total)).astype(jnp.bfloat16)


def combine_sums(earlier, following):
    return earlier + following


def per_device(coeffs, legendre, slot_wave, lon_points, quad_weights):
    slot_count = coeffs.shape[0]
    fields = coeffs.shape[2]
    lev_local = coeffs.shape[3]
    wave_total = coeffs.shape[4]
    wave_count = lax.axis_size("wave")
    north_count = legendre.shape[2]
    lat_total = 2 * north_count
    lat_dev = lat_total // wave_count
    channels = 2 * fields * lev_local
    half_count = fields * lev_local
    levels_all = lev_local * lax.axis_size("lev")
    device = lax.axis_index("wave")
    waves_local = lax.dynamic_slice_in_dim(slot_wave, device * slot_count, slot_count)
    spectral = coeffs.reshape(slot_count, channels, wave_total)
    north_four, south_four = padded_inverse(spectral, legendre, waves_local)
    outgoing = jnp.concatenate([north_four, south_four[:, ::-1]], axis=1)
    latitudes = device * lat_dev + jnp.arange(lat_dev, dtype=jnp.int32)
    incoming = lax.all_to_all(outgoing, "wave", split_axis=1, concat_axis=2, tiled=True)
    fourier = incoming.transpose(1, 0, 2)
    points_all = lon_points[latitudes]
    blocks = (4 * wave_total + 16 + block_width - 1) // block_width
    grouped = fourier.reshape(lat_dev, 1, channels, wave_total)

    def grid_group(operands):
        rows, points = operands
        tables = transform_tables(slot_wave, points, blocks)
        return to_grid(rows, tables, points, slot_wave)

    grid_field = lax.map(grid_group, (grouped, points_all))
    group_count = grid_field.shape[0]
    group_size = grid_field.shape[1]
    span = grid_field.shape[3]
    field_grid = grid_field.reshape(group_count, group_size, fields, lev_local, span)
    mass_local = jnp.cumsum(field_grid[:, :, 1], axis=2)
    heat_local = jnp.cumsum(field_grid[:, :, 2], axis=2)
    totals = jnp.stack([mass_local[:, :, -1], heat_local[:, :, -1]])
    lower_sums = prefix(totals, "lev", combine_sums, jnp.zeros_like(totals))
    level_scale = 1.0 / math.sqrt(levels_all)
    mass_sum = (mass_local + lower_sums[0][:, :, None]) * level_scale
    geopot = (heat_local + lower_sums[1][:, :, None]) * level_scale
    forcing = jnp.stack(
        [
            field_grid[:, :, 0] * field_grid[:, :, 1],
            geopot,
            field_grid[:, :, 2] * mass_sum,
            field_grid[:, :, 3] + mass_sum,
        ],
        axis=2,
    )
    forcing = forcing.reshape(group_count, group_size, half_count, span)

    def spectral_group(operands):
        forcing_rows, points = operands
        tables = transform_tables(slot_wave, points, blocks)
        return to_spectral(forcing_rows, tables, points, slot_wave)

    spectral_rows = lax.map(spectral_group, (forcing, points_all))
    spectral_rows = spectral_rows.reshape(lat_dev, channels, wave_total)
    weighted = (
        (quad_weights[latitudes][:, None, None] * spectral_rows)
        .astype(jnp.bfloat16)
        .transpose(1, 0, 2)
    )
    returned = lax.all_to_all(weighted, "wave", split_axis=2, concat_axis=1, tiled=True)
    north_grid = returned[:, :north_count]
    south_grid = returned[:, north_count:][:, ::-1]
    result = padded_direct(north_grid, south_grid, legendre, waves_local, lat_total)
    return result.reshape(coeffs.shape)


def solution(mesh):
    placed = (P("wave", None, None, "lev", None), P("wave", None, None), P(), P(), P())
    return jax.shard_map(
        per_device,
        mesh=mesh,
        in_specs=placed,
        out_specs=P("wave", None, None, "lev", None),
        check_vma=False,
    )
```

profile of v0, /device:TPU:1, one launch (start us, length us, event | category | flops | bytes accessed | tf_op | source)
XLA Modules:
  0.0 643.5 jit_solution(2573593360882004559)
XLA Ops:
  4.0 2.3 fusion.55
  7.7 2.7 reverse.3
  13.2 3.1 copy.25
  16.3 3.6 reshape.609
  19.9 21.0 %all-to-all-start = ((f32[128,1,1152]{2,1,0:T(1,128)}), f32[128,1,1152]{2,1,0:T(1,128)}, u32[]{:S(2)}, u32[]{:S(2)}) async-start(f32[128,1,1152]{2,1,0:T(1,128)} %reshape.609), calls=%async_computation | async-start | bytes 1179648 | tf_op jit(solution)/shard_map/all_to_all | solution.py:135
  42.2 32.1 %all-to-all-done = f32[128,1,1152]{2,1,0:T(1,128)} async-done(((f32[128,1,1152]{2,1,0:T(1,128)}), f32[128,1,1152]{2,1,0:T(1,128)}, u32[]{:S(2)}, u32[]{:S(2)}) %all-to-all-start) | async-done | bytes 589856 | tf_op jit(solution)/shard_map/all_to_all | solution.py:135
  74.7 3.9 reduce.12
  78.7 3.2 reshape.610
  81.9 3.8 copy.27
  85.7 4.0 all_to_all.29
  89.7 3.2 copy.28
  92.8 233.8 %while.40 = (s32[]{:T(128)}, f32[6,1,16,3584]{3,0,2,1:T(8,128)}, s32[768]{0:T(1024)S(1)}, s32[6]{0:T(128)S(1)}, f32[6,1,32,768]{3,2,1,0:T(8,128)}, /*index=5*/s3...) while((s32[]{:T(128)}, f32[6,1,16,3584]{3,0,2,1:T(8,128)}, s32[768]{0:T(1024)S(1)}, s32[6]{0:T(128)S(1)}, ...), condition=%wide.region_1.2_spmd, body=%wide.region_0.1_spmd.sunk | while | flops 1062911232 | bytes 10812844 | solution.py:146
  99.2 20.8 %fusion.100 = (f32[768,512]{1,0:T(8,128)S(1)}, f32[768,512]{1,0:T(8,128)S(1)}) fusion(f32[]{:T(128)S(6)} %div.86, s32[]{:T(128)S(6)} %select_n.240, s32[768]{0:T(1024)S(1)} %get-tuple-element.493, pred[]{:T(512)S(6)} %lt.204), kind=kLoop, calls=%fused_computation.13.clone.1 | loop fusion | flops 4325376 | bytes 3148809 | tf_op jit(solution)/shard_map/while/body/eval_jaxpr/cos | solution.py:29
  120.0 1.9 fusion.103
  127.1 4.9 dynamic_update_slice.19
  138.1 20.8 %fusion.100 = (f32[768,512]{1,0:T(8,128)S(1)}, f32[768,512]{1,0:T(8,128)S(1)}) fusion(f32[]{:T(128)S(6)} %div.86, s32[]{:T(128)S(6)} %select_n.240, s32[768]{0:T(1024)S(1)} %get-tuple-element.493, pred[]{:T(512)S(6)} %lt.204), kind=kLoop, calls=%fused_computation.13.clone.1 | loop fusion | flops 4325376 | bytes 3148809 | tf_op jit(solution)/shard_map/while/body/eval_jaxpr/cos | solution.py:29
  159.0 1.9 fusion.103
  166.0 4.9 dynamic_update_slice.19
  177.1 20.8 %fusion.100 = (f32[768,512]{1,0:T(8,128)S(1)}, f32[768,512]{1,0:T(8,128)S(1)}) fusion(f32[]{:T(128)S(6)} %div.86, s32[]{:T(128)S(6)} %select_n.240, s32[768]{0:T(1024)S(1)} %get-tuple-element.493, pred[]{:T(512)S(6)} %lt.204), kind=kLoop, calls=%fused_computation.13.clone.1 | loop fusion | flops 4325376 | bytes 3148809 | tf_op jit(solution)/shard_map/while/body/eval_jaxpr/cos | solution.py:29
  197.9 1.9 fusion.103
  204.9 4.9 dynamic_update_slice.19
  216.0 20.8 %fusion.100 = (f32[768,512]{1,0:T(8,128)S(1)}, f32[768,512]{1,0:T(8,128)S(1)}) fusion(f32[]{:T(128)S(6)} %div.86, s32[]{:T(128)S(6)} %select_n.240, s32[768]{0:T(1024)S(1)} %get-tuple-element.493, pred[]{:T(512)S(6)} %lt.204), kind=kLoop, calls=%fused_computation.13.clone.1 | loop fusion | flops 4325376 | bytes 3148809 | tf_op jit(solution)/shard_map/while/body/eval_jaxpr/cos | solution.py:29
  236.8 1.9 fusion.103
  243.8 4.9 dynamic_update_slice.19
  254.9 20.8 %fusion.100 = (f32[768,512]{1,0:T(8,128)S(1)}, f32[768,512]{1,0:T(8,128)S(1)}) fusion(f32[]{:T(128)S(6)} %div.86, s32[]{:T(128)S(6)} %select_n.240, s32[768]{0:T(1024)S(1)} %get-tuple-element.493, pred[]{:T(512)S(6)} %lt.204), kind=kLoop, calls=%fused_computation.13.clone.1 | loop fusion | flops 4325376 | bytes 3148809 | tf_op jit(solution)/shard_map/while/body/eval_jaxpr/cos | solution.py:29
  275.7 1.9 fusion.103
  282.8 4.9 dynamic_update_slice.19
  293.8 20.8 %fusion.100 = (f32[768,512]{1,0:T(8,128)S(1)}, f32[768,512]{1,0:T(8,128)S(1)}) fusion(f32[]{:T(128)S(6)} %div.86, s32[]{:T(128)S(6)} %select_n.240, s32[768]{0:T(1024)S(1)} %get-tuple-element.493, pred[]{:T(512)S(6)} %lt.204), kind=kLoop, calls=%fused_computation.13.clone.1 | loop fusion | flops 4325376 | bytes 3148809 | tf_op jit(solution)/shard_map/while/body/eval_jaxpr/cos | solution.py:29
  314.7 1.9 fusion.103
  321.7 4.9 dynamic_update_slice.19
  329.8 11.6 %all_gather.4 = bf16[4,2,6,1,3584]{4,1,3,2,0:T(2,128)(2,1)} all-gather(bf16[1,2,6,1,3584]{4,1,3,2,0:T(2,128)(2,1)S(1)} %copy.30), channel_id=1, replica_groups=mesh['wave'=128,'lev'=4] {'lev'}, dimensions={0}, use_global_device_ids=true | all-gather | bytes 430080 | tf_op jit(solution)/shard_map/all_gather | solution.py:15
  341.4 13.7 %while.42 = (s32[]{:T(128)}, f32[2,6,1,3584]{3,2,1,0:T(1,128)}, s32[]{:T(128)}, bf16[4,2,6,1,3584]{4,1,3,2,0:T(2,128)(2,1)}, s32[]{:T(128)}, /*index=5*/s32[]{:T(128)}) while((s32[]{:T(128)}, f32[2,6,1,3584]{3,2,1,0:T(1,128)}, s32[]{:T(128)}, bf16[4,2,6,1,3584]{4,1,3,2,0:T(2,128)(2,1)}, s32[]{:T(128)}, /*index=5*/s32[]{:T(128)}) %tuple.117), condition=%wide.region_5.6_spmd.clone, body=%wide.region_4.5_spmd.clone.sunk | while | flops 172036 | bytes 602205 | solution.py:23
  346.4 1.9 broadcast_select_fusion.6
  349.8 1.9 broadcast_select_fusion.6
  360.3 210.4 %while.41 = (s32[]{:T(128)}, f32[6,1,32,768]{3,2,1,0:T(8,128)}, s32[768]{0:T(1024)S(1)}, s32[6]{0:T(128)S(1)}, f32[6,1,16,3584]{3,0,2,1:T(8,128)}, /*index=5*/s3...) while((s32[]{:T(128)}, f32[6,1,32,768]{3,2,1,0:T(8,128)}, s32[768]{0:T(1024)S(1)}, s32[6]{0:T(128)S(1)}, ...), condition=%wide.region_9.10_spmd, body=%wide.region_6.9_spmd.sunk | while | flops 1062845184 | bytes 8753064 | solution.py:174
  380.0 20.8 %fusion.106 = (f32[768,512]{1,0:T(8,128)S(1)}, f32[768,512]{1,0:T(8,128)S(1)}) fusion(f32[]{:T(128)S(6)} %div.92, s32[]{:T(128)S(6)} %select_n.244, s32[768]{0:T(1024)S(1)} %get-tuple-element.541, pred[]{:T(512)S(6)} %lt.207), kind=kLoop, calls=%fused_computation.60.clone.1 | loop fusion | flops 4325376 | bytes 3148809 | tf_op jit(solution)/shard_map/while/body/eval_jaxpr/cos | solution.py:29
  400.8 2.1 dynamic-slice_reduce_fusion.2
  403.0 3.3 fusion.107
  412.2 20.8 %fusion.106 = (f32[768,512]{1,0:T(8,128)S(1)}, f32[768,512]{1,0:T(8,128)S(1)}) fusion(f32[]{:T(128)S(6)} %div.92, s32[]{:T(128)S(6)} %select_n.244, s32[768]{0:T(1024)S(1)} %get-tuple-element.541, pred[]{:T(512)S(6)} %lt.207), kind=kLoop, calls=%fused_computation.60.clone.1 | loop fusion | flops 4325376 | bytes 3148809 | tf_op jit(solution)/shard_map/while/body/eval_jaxpr/cos | solution.py:29
  433.0 2.1 dynamic-slice_reduce_fusion.2
  435.2 3.3 fusion.107
  444.4 20.8 %fusion.106 = (f32[768,512]{1,0:T(8,128)S(1)}, f32[768,512]{1,0:T(8,128)S(1)}) fusion(f32[]{:T(128)S(6)} %div.92, s32[]{:T(128)S(6)} %select_n.244, s32[768]{0:T(1024)S(1)} %get-tuple-element.541, pred[]{:T(512)S(6)} %lt.207), kind=kLoop, calls=%fused_computation.60.clone.1 | loop fusion | flops 4325376 | bytes 3148809 | tf_op jit(solution)/shard_map/while/body/eval_jaxpr/cos | solution.py:29
  465.2 2.1 dynamic-slice_reduce_fusion.2
  467.4 3.3 fusion.107
  476.6 20.8 %fusion.106 = (f32[768,512]{1,0:T(8,128)S(1)}, f32[768,512]{1,0:T(8,128)S(1)}) fusion(f32[]{:T(128)S(6)} %div.92, s32[]{:T(128)S(6)} %select_n.244, s32[768]{0:T(1024)S(1)} %get-tuple-element.541, pred[]{:T(512)S(6)} %lt.207), kind=kLoop, calls=%fused_computation.60.clone.1 | loop fusion | flops 4325376 | bytes 3148809 | tf_op jit(solution)/shard_map/while/body/eval_jaxpr/cos | solution.py:29
  497.4 2.1 dynamic-slice_reduce_fusion.2
  499.5 3.3 fusion.107
  508.7 20.8 %fusion.106 = (f32[768,512]{1,0:T(8,128)S(1)}, f32[768,512]{1,0:T(8,128)S(1)}) fusion(f32[]{:T(128)S(6)} %div.92, s32[]{:T(128)S(6)} %select_n.244, s32[768]{0:T(1024)S(1)} %get-tuple-element.541, pred[]{:T(512)S(6)} %lt.207), kind=kLoop, calls=%fused_computation.60.clone.1 | loop fusion | flops 4325376 | bytes 3148809 | tf_op jit(solution)/shard_map/while/body/eval_jaxpr/cos | solution.py:29
  529.6 2.1 dynamic-slice_reduce_fusion.2
  531.7 3.3 fusion.107
  540.9 20.8 %fusion.106 = (f32[768,512]{1,0:T(8,128)S(1)}, f32[768,512]{1,0:T(8,128)S(1)}) fusion(f32[]{:T(128)S(6)} %div.92, s32[]{:T(128)S(6)} %select_n.244, s32[768]{0:T(1024)S(1)} %get-tuple-element.541, pred[]{:T(512)S(6)} %lt.207), kind=kLoop, calls=%fused_computation.60.clone.1 | loop fusion | flops 4325376 | bytes 3148809 | tf_op jit(solution)/shard_map/while/body/eval_jaxpr/cos | solution.py:29
  561.7 2.1 dynamic-slice_reduce_fusion.2
  563.9 3.3 fusion.107
  570.7 3.1 copy.33
  573.8 3.3 fusion.84
  577.1 3.4 reshape.611
  580.5 34.0 %all_to_all.36 = bf16[128,2,576]{2,1,0:T(2,128)(2,1)} all-to-all(bf16[128,2,576]{2,1,0:T(2,128)(2,1)} %reshape.611), channel_id=1, replica_groups=mesh['wave'=128,'lev'=4] {'wave'}, dimensions={0} | all-to-all | bytes 589824 | tf_op jit(solution)/shard_map/all_to_all | solution.py:181
  614.5 3.5 reshape.612
  618.0 2.8 copy.35
  620.8 3.3 all_to_all.33
  624.1 1.9 slice.87
  626.0 3.1 fusion.56
  629.2 9.1 %rev.7 = bf16[32,384,6]{0,1,2:T(8,128)(2,1)} reverse(bf16[32,384,6]{0,1,2:T(8,128)(2,1)} %slice.87), dimensions={1} | reverse | bytes 294912 | tf_op jit(solution)/shard_map/rev | solution.py:183
  638.3 3.2 fusion.54
  (159 shorter events, 101.5 us)
Async XLA Ops:
  0.0 4.0 copy-start
  4.0 2.4 copy-start.4
  4.0 2.4 copy-start.8
  16.3 24.6 %copy-start.1 = (s32[768]{0:T(1024)S(1)}, s32[768]{0:T(1024)}, u32[]{:S(2)}) copy-start(s32[768]{0:T(1024)} %param.14) | copy-start | bytes 9220
  16.3 25.2 %copy-start.2 = (f32[768]{0:T(1024)S(1)}, f32[768]{0:T(1024)}, u32[]{:S(2)}) copy-start(f32[768]{0:T(1024)} %param.15) | copy-start | bytes 9220
  19.9 54.4 %all-to-all-start = ((f32[128,1,1152]{2,1,0:T(1,128)}), f32[128,1,1152]{2,1,0:T(1,128)}, u32[]{:S(2)}, u32[]{:S(2)}) async-start(f32[128,1,1152]{2,1,0:T(1,128)} %reshape.609), calls=%async_computation | async-start | bytes 1179648 | tf_op jit(solution)/shard_map/all_to_all | solution.py:135
  89.7 3.2 copy-start.3
  327.7 2.0 copy-start.6
  328.9 0.8 copy-start.5
  355.1 2.1 copy-start.7
where the time goes:
time: 656 us; the launch traced here: 644 us
  other arithmetic  313 us (48%)
  local copies, waits for them, and re-layouts  141 us (21%)
  loops' own time  49.4 us (8%)
  blocking collectives  45.6 us (7%)
  matrix products  40.9 us (6%)
  waiting for transfers between devices  32.1 us (5%)
  starting transfers between devices  21 us (3%)
    cos x24, other arithmetic, angle_pair(): return (jnp.cos(angles), jnp.sin(angles))  255 us
    dynamic_update_slice x12, local copies, waits for them, and re-layouts, per_device(): grid_field = lax.map(grid_group, (grouped, points_all))  35 us
    all_to_all x1, blocking collectives, per_device(): lax.all_to_all(weighted, 'wave', split_axis=2, concat_axis=1, tiled=True)  34 us
    another operation x1, loops' own time, per_device(): spectral_rows = lax.map(spectral_group, (forcing, points_all))  33.3 us
    all_to_all x1, waiting for transfers between devices, per_device(): lax.all_to_all(outgoing, 'wave', split_axis=1, concat_axis=2, tiled=True)  32.1 us
    all_to_all x1, starting transfers between devices, per_device(): lax.all_to_all(outgoing, 'wave', split_axis=1, concat_axis=2, tiled=True)  21 us
    dot_general x6, matrix products, to_spectral(): jnp.einsum('lcbq,sq->lbcs', shaped, base_table, precision=highest)  19.6 us
    another operation x1, loops' own time, per_device(): grid_field = lax.map(grid_group, (grouped, points_all))  16.1 us
  transfers between devices with their start and end apart: 1, of which 1 were waited for; matrix products, arithmetic and copies ran while one was open for 0% of the time, Pallas kernels for 0%

commit v1 on v0

v1 whole, which is shorter than its diff:
```python
import math

import numpy as np
import jax
import jax.numpy as jnp
from jax import lax
from jax.experimental import pallas as pl
from jax.experimental.pallas import tpu as pltpu
from jax.sharding import PartitionSpec as P

MESH = pl.DeviceIdType.MESH
f32 = jnp.float32
bf16 = jnp.bfloat16
SLOTS = 6
DEGREES = 768
HALF = 384
WAVE = 128
LEV = 4
LATS = 3
LANES = 128
WIDTH = 512
ROOT = 1.0 / math.sqrt(768.0)


def turn_polynomials(terms):
    x = np.cos(np.linspace(0.0, np.pi, 4001)) * 0.5
    y = x * x
    powers = np.stack([y**i for i in range(terms)], axis=1)
    cosine = np.linalg.lstsq(powers, np.cos(2 * np.pi * x), rcond=None)[0]
    sine = np.linalg.lstsq(powers * x[:, None], np.sin(2 * np.pi * x), rcond=None)[0]
    return [float(np.float32(c)) for c in cosine], [float(np.float32(c)) for c in sine]


COSINE, SINE = turn_polynomials(6)


def horner(coefficients, y):
    total = coefficients[-1]
    for c in coefficients[-2::-1]:
        total = total * y + c
    return total


def kernel(
    lon_s, slot_s, quad_s, waves_ref, lat_ref, coeffs_ref, legendre_ref, out_ref,
    sums, lev_send, lev_recv, lower, stage, four, column, tables, planes, wide,
    send_one, recv_one, send_two, recv_two, pairs, left, sumpq, leftback, planes_two, weighted,
    lev_ssem, lev_rsem, ssem_one, rsem_one, ssem_two, rsem_two,
):
    me = lax.axis_index("wave")
    lev = lax.axis_index("lev")
    barrier = pltpu.get_barrier_semaphore()

    def greet(i, carry):
        pl.semaphore_signal(barrier, inc=1, device_id=(lax.rem(me + i, WAVE), lev), device_id_type=MESH)
        return carry

    lax.fori_loop(1, WAVE, greet, 0)
    for i in range(1, LEV):
        pl.semaphore_signal(barrier, inc=1, device_id=(me, lax.rem(lev + i, LEV)), device_id_type=MESH)

    sums[24:32, :] = jnp.zeros((8, DEGREES), f32)
    for s in range(SLOTS):
        for r in range(2):
            for f in (1, 2):
                row = s * 4 + r * 2 + f - 1
                sums[row : row + 1, :] = jnp.sum(coeffs_ref[s, r, f].astype(f32), axis=0, keepdims=True)
    lev_send[...] = sums[...].astype(bf16)
    lev_recv[lev] = jnp.zeros((32, DEGREES), bf16)
    pl.semaphore_wait(barrier, WAVE - 1 + LEV - 1)
    for i in range(1, LEV):
        pltpu.make_async_remote_copy(
            src_ref=lev_send, dst_ref=lev_recv.at[lev], send_sem=lev_ssem, recv_sem=lev_rsem,
            device_id=(me, lax.rem(lev + i, LEV)), device_id_type=MESH,
        ).start()

    for q in range(3):
        first = waves_ref[2 * q : 2 * q + 1, :]
        second = waves_ref[2 * q + 1 : 2 * q + 2, :]
        even_first = (first & 1) == 0
        even = jnp.where(even_first, first, second)
        odd = jnp.where(even_first, second, first)
        column[q] = jnp.broadcast_to(even.astype(f32), (LANES, LANES)).T
        column[3 + q] = jnp.broadcast_to(odd.astype(f32), (LANES, LANES)).T

    def table_block(step, carry):
        t = step // 6
        c = lax.rem(step, 6)
        parity = c // 3
        q = lax.rem(c, 3)
        points = lon_s[me + LANES * t]
        per_point = 1.0 / jnp.full((1, LANES), points, jnp.int32).astype(f32)
        wave = column[c]
        lane = lax.broadcasted_iota(jnp.int32, (1, LANES), 1).astype(f32)
        for block in range(WIDTH // LANES):
            turn = wave * (lane + float(block * LANES)) * per_point
            x = turn - jnp.floor(turn + 0.5)
            y = x * x
            rows = pl.ds(pl.multiple_of(q * LANES, LANES), LANES)
            columns = pl.ds(block * LANES, LANES)
            tables[t, 2 * parity, rows, columns] = horner(COSINE, y).astype(bf16)
            tables[t, 2 * parity + 1, rows, columns] = (horner(SINE, y) * x).astype(bf16)
        return carry

    lax.fori_loop(0, LATS * 6, table_block, 0)

    everyone = pltpu.make_async_copy(lev_recv.at[pl.ds(0, LEV - 1)], lev_recv.at[pl.ds(0, LEV - 1)], lev_rsem)
    everyone.wait()
    pltpu.make_async_copy(lev_recv.at[pl.ds(0, LEV - 1)], lev_recv.at[pl.ds(0, LEV - 1)], lev_ssem).wait()
    total = jnp.zeros((32, DEGREES), f32)
    for k in range(LEV):
        total = total + jnp.where(k < lev, lev_recv[k].astype(f32), 0.0)
    sums[...] = total
    for s in range(SLOTS):
        lower[s, 0:4, :] = sums[s * 4 : s * 4 + 4, :]

    degree = lax.broadcasted_iota(jnp.int32, (1, DEGREES), 1)
    place = (0, 4, 2, 6)
    for b in range(DEGREES // LANES):
        stage[b, 72:80, :] = jnp.zeros((8, LANES), f32)

    def put_rows(start, stride, value):
        for b in range(DEGREES // LANES):
            stage[b, pl.ds(start, 4, stride=stride), :] = value[:, b * LANES : (b + 1) * LANES]

    def forward(s, carry):
        m = slot_s[me * SLOTS + s]
        keep = (degree >= m).astype(f32)
        flipped = keep * (1.0 - 2.0 * ((degree + m) & 1).astype(f32))
        for r in range(2):
            for f in range(4):
                value = coeffs_ref[s, r, f].astype(f32)
                put_rows(r * 32 + place[f], 8, value * keep)
                put_rows(r * 32 + place[f] + 1, 8, value * flipped)
        extra = lower[s, 0:4, :]
        put_rows(64, 2, extra * keep)
        put_rows(65, 2, extra * flipped)
        operand = jnp.concatenate([stage[b] for b in range(DEGREES // LANES)], axis=1).astype(bf16)
        product = jnp.dot(operand, legendre_ref[s], preferred_element_type=f32) * ROOT
        for t in range(LATS):
            four[s, t] = product[:, t * LANES : (t + 1) * LANES]
        return carry

    lax.fori_loop(0, SLOTS, forward, 0)

    def spread(step, carry):
        r = step // 4
        v = lax.rem(step, 4)
        for t in range(LATS):
            for j in range(SLOTS):
                base = (t * SLOTS + j) * 7
                planes[step, base : base + 7, :] = four[j, t, pl.ds(pl.multiple_of(step * 8, 8), 8), :][0:7]
        planes[step, 126:128, :] = jnp.zeros((2, LANES), f32)
        return carry

    lax.fori_loop(0, 8, spread, 0)
    for r in range(2):
        for ns in range(2):
            for t in range(LATS):
                for j in range(SLOTS):
                    base = (t * SLOTS + j) * 7 + 6
                    row = 64 + r * 4 + ns
                    planes[r * 4 + ns, base : base + 1, :] = four[j, t, row : row + 1, :]
    for rv in range(8):
        wide[pl.ds(rv, LANES, stride=8), :] = planes[rv].T

    def narrow_one(i, carry):
        rows = pl.ds(pl.multiple_of(i * 128, 128), 128)
        send_one[pl.ds(i * 16, 16)] = wide[rows, :].reshape(16, 8, LANES).astype(bf16)
        return carry

    lax.fori_loop(0, 8, narrow_one, 0)

    def exchange(outgoing, incoming, ssem, rsem):
        pltpu.make_async_copy(outgoing.at[me], incoming.at[me], rsem).start()

        def put(peer):
            pltpu.make_async_remote_copy(
                src_ref=outgoing.at[peer], dst_ref=incoming.at[me], send_sem=ssem, recv_sem=rsem,
                device_id=(peer, lev), device_id_type=MESH,
            ).start()

        put(lax.rem(me + WAVE // 2, WAVE))

        def both(i, carry):
            put(lax.rem(me + WAVE // 2 - i, WAVE))
            put(lax.rem(me + WAVE // 2 + i, WAVE))
            return carry

        lax.fori_loop(1, WAVE // 2, both, 0)

    def settle(outgoing, incoming, ssem, rsem):
        pltpu.make_async_copy(incoming, incoming, rsem).wait()
        part = outgoing.at[pl.ds(0, WAVE - 1)]
        pltpu.make_async_copy(part, part, ssem).wait()

    exchange(send_one, recv_one, ssem_one, rsem_one)

    def level_sum(value, first, second):
        row = lax.broadcasted_iota(jnp.int32, value.shape, 0)
        level = row & 3
        value = value + jnp.where(level >= 1, pltpu.roll(value, 1, 0), 0.0)
        value = value + jnp.where(level >= 2, pltpu.roll(value, 2, 0), 0.0)
        return (value + jnp.where(row < 4, first, second)) * 0.25

    def local(s, carry):
        m = slot_s[me * SLOTS + s]
        row = lax.broadcasted_iota(jnp.int32, (8, LANES), 0)
        live = jnp.where((row < 4) | (m > 0), 1.0, 0.0)
        for t in range(LATS):
            columns = slice(t * LANES, (t + 1) * LANES)
            inside = (2.0 * m.astype(f32) < lat_ref[0:1, columns]).astype(f32)
            for ns in range(2):
                factor = live * (inside * lat_ref[1 + ns : 2 + ns, columns])

                def rows(place, low):
                    return level_sum(
                        four[s, t, pl.ds(place + ns, 8, stride=8), :],
                        four[s, t, low + ns : low + ns + 1, :],
                        four[s, t, low + ns + 4 : low + ns + 5, :],
                    )

                weighted[s, t, ns * 16 + 8 : ns * 16 + 16, :] = rows(2, 66) * factor
                weighted[s, t, 32 + ns * 16 + 8 : 32 + ns * 16 + 16, :] = (
                    four[s, t, pl.ds(6 + ns, 8, stride=8), :] + rows(4, 64)
                ) * factor
        return carry

    lax.fori_loop(0, SLOTS, local, 0)

    settle(send_one, recv_one, ssem_one, rsem_one)

    def widen(incoming):
        def body(i, carry):
            rows = pl.ds(pl.multiple_of(i * 128, 128), 128)
            wide[rows, :] = incoming[pl.ds(i * 16, 16)].astype(f32).reshape(128, LANES)
            return carry

        lax.fori_loop(0, 8, body, 0)
        for rv in range(8):
            planes[rv] = wide[pl.ds(rv, LANES, stride=8), :].T

    widen(recv_one)

    for t in range(LATS):
        points = jnp.full((1, LANES), lon_s[me + LANES * t], jnp.int32)
        for r in range(2):
            for j in range(SLOTS):
                base = (t * SLOTS + j) * 7
                for v in range(4):
                    rv = r * 4 + v
                    pairs[r, j, v * 4 : v * 4 + 4, :] = planes[rv, base : base + 4, :]
                    pairs[r, j, 16 + v * 4 : 18 + v * 4, :] = planes[rv, base + 4 : base + 6, :]
                for ns in range(2):
                    run = planes[r * 4 + ns, base + 6 : base + 7, :]
                    for v in range(4):
                        run = run + planes[r * 4 + v, base + 4 + ns : base + 5 + ns, :]
                        row = 18 + v * 4 + ns
                        pairs[r, j, row : row + 1, :] = run * 0.25
        for q in range(3):
            first = waves_ref[2 * q : 2 * q + 1, :]
            second = waves_ref[2 * q + 1 : 2 * q + 2, :]
            even_first = (first & 1) == 0
            even = jnp.where(even_first, first, second)
            odd = jnp.where(even_first, second, first)
            sigma = 1.0 - (even & 2).astype(f32)
            tau = 1.0 - (odd & 2).astype(f32)
            even_factor = jnp.where(2 * even < points, jnp.where(even == 0, 1.0, 2.0), 0.0)
            odd_factor = jnp.where(2 * odd < points, 2.0, 0.0)
            pick = jnp.broadcast_to(even_first.astype(f32), (32, LANES)) > 0.5
            columns = slice(q * LANES, (q + 1) * LANES)
            real_even = jnp.where(pick, pairs[0, 2 * q], pairs[0, 2 * q + 1]) * even_factor
            real_odd = jnp.where(pick, pairs[0, 2 * q + 1], pairs[0, 2 * q]) * odd_factor
            imag_even = jnp.where(pick, pairs[1, 2 * q], pairs[1, 2 * q + 1]) * even_factor
            imag_odd = jnp.where(pick, pairs[1, 2 * q + 1], pairs[1, 2 * q]) * odd_factor
            left[t, 0, 0:32, columns] = real_even.astype(bf16)
            left[t, 0, 32:64, columns] = (sigma * real_even).astype(bf16)
            left[t, 1, 0:32, columns] = imag_even.astype(bf16)
            left[t, 1, 32:64, columns] = (sigma * imag_even).astype(bf16)
            left[t, 2, 0:32, columns] = real_odd.astype(bf16)
            left[t, 2, 32:64, columns] = (tau * imag_odd).astype(bf16)
            left[t, 3, 0:32, columns] = imag_odd.astype(bf16)
            left[t, 3, 32:64, columns] = (tau * real_odd).astype(bf16)

    def latitude(t, carry):
        whole_points = lon_s[me + LANES * t]
        for i in range(4):
            sumpq[i] = jnp.dot(left[t, i], tables[t, i], preferred_element_type=f32)
        lane = lax.broadcasted_iota(jnp.int32, (1, LANES), 1)
        for block in range(WIDTH // LANES):
            columns = slice(block * LANES, (block + 1) * LANES)
            k = lane + block * LANES
            points = jnp.full((1, LANES), whole_points, jnp.int32)
            share = jnp.where(8 * k < points, 1.0, jnp.where(8 * k == points, 0.5, 0.0))
            share = jnp.where(k == 0, 0.5, share)
            even_p, turn_p = sumpq[0, 0:32, columns], sumpq[0, 32:64, columns]
            even_m, turn_m = sumpq[1, 0:32, columns], sumpq[1, 32:64, columns]
            odd_p, side_m = sumpq[2, 0:32, columns], sumpq[2, 32:64, columns]
            odd_m, side_p = sumpq[3, 0:32, columns], sumpq[3, 32:64, columns]

            def product(grid):
                return grid[0:16] * grid[16:32] * share

            a, b = even_p - even_m, odd_p - odd_m
            f0p, f2p = product(a + b), product(a - b)
            a, b = even_p + even_m, odd_p + odd_m
            f0m, f2m = product(a + b), product(a - b)
            a, b = turn_p - turn_m, side_p + side_m
            f3p, f1p = product(a + b), product(a - b)
            a, b = turn_p + turn_m, side_p - side_m
            f1m, f3m = product(a + b), product(a - b)
            a, b = f0p + f2p, f0m + f2m
            leftback[0, 0:16, columns] = (a + b).astype(bf16)
            leftback[1, 0:16, columns] = (a - b).astype(bf16)
            a, b = f1p + f3p, f1m + f3m
            leftback[0, 16:32, columns] = (a + b).astype(bf16)
            leftback[1, 16:32, columns] = (a - b).astype(bf16)
            a, b = f0p - f2p, f0m - f2m
            leftback[2, 0:16, columns] = (a + b).astype(bf16)
            leftback[3, 0:16, columns] = (a - b).astype(bf16)
            a, b = f1p - f3p, f1m - f3m
            leftback[2, 16:32, columns] = (a + b).astype(bf16)
            leftback[3, 16:32, columns] = (b - a).astype(bf16)
        for i in range(4):
            sumpq[i, 0:32, 0:HALF] = lax.dot_general(
                leftback[i], tables[t, i], (((1,), (1,)), ((), ())), preferred_element_type=f32
            )
        north = quad_s[me + LANES * t]
        south = quad_s[2 * HALF - 1 - me - LANES * t]
        row = lax.broadcasted_iota(jnp.int32, (16, LANES), 0)
        points = jnp.full((1, LANES), whole_points, jnp.int32)
        weight = jnp.where((row & 1) == 0, north, south) * (ROOT / points.astype(f32))
        for q in range(3):
            first = waves_ref[2 * q : 2 * q + 1, :]
            second = waves_ref[2 * q + 1 : 2 * q + 2, :]
            even_first = (first & 1) == 0
            even = jnp.where(even_first, first, second)
            odd = jnp.where(even_first, second, first)
            sigma = 1.0 - (even & 2).astype(f32)
            tau = 1.0 - (odd & 2).astype(f32)
            even_weight = weight * (2 * even < points).astype(f32)
            odd_weight = weight * (2 * odd < points).astype(f32)
            pick = jnp.broadcast_to(even_first.astype(f32), (16, LANES)) > 0.5
            columns = slice(q * LANES, (q + 1) * LANES)
            real_even = (sumpq[0, 0:16, columns] + sigma * sumpq[0, 16:32, columns]) * even_weight
            imag_even = (sumpq[1, 0:16, columns] + sigma * sumpq[1, 16:32, columns]) * -even_weight
            real_odd = (sumpq[2, 0:16, columns] + tau * sumpq[3, 16:32, columns]) * odd_weight
            imag_odd = (sumpq[3, 0:16, columns] + tau * sumpq[2, 16:32, columns]) * -odd_weight
            for r, one, two in ((0, real_even, real_odd), (1, imag_even, imag_odd)):
                for j, value in ((2 * q, jnp.where(pick, one, two)), (2 * q + 1, jnp.where(pick, two, one))):
                    for v in range(4):
                        planes_two[r * 4 + v, t, j * 4 : j * 4 + 4, :] = value[v * 4 : v * 4 + 4]
        return carry

    lax.fori_loop(0, LATS, latitude, 0)

    for rv in range(8):
        filled = planes_two[rv].reshape(LATS * 24, LANES)
        square = jnp.concatenate([filled, jnp.zeros((LANES - LATS * 24, LANES), f32)], axis=0)
        wide[pl.ds(rv, LANES, stride=8), :] = square.T

    def narrow_two(i, carry):
        rows = pl.ds(pl.multiple_of(i * 128, 128), 128)
        send_two[pl.ds(i * 16, 16)] = wide[rows, :].reshape(16, 8, LANES).astype(bf16)
        return carry

    lax.fori_loop(0, 8, narrow_two, 0)
    exchange(send_two, recv_two, ssem_two, rsem_two)
    settle(send_two, recv_two, ssem_two, rsem_two)
    widen(recv_two)
    for rv in range(8):
        for t in range(LATS):
            for j in range(SLOTS):
                base = (t * SLOTS + j) * 4
                weighted[j, t, pl.ds(rv, 4, stride=16), :] = planes[rv, base : base + 4, :]

    def direct(s, carry):
        m = slot_s[me * SLOTS + s]
        keep = (degree >= m).astype(f32) * ROOT
        flipped = keep * (1.0 - 2.0 * ((degree + m) & 1).astype(f32))
        operand = jnp.concatenate([weighted[s, t] for t in range(LATS)], axis=1).astype(bf16)
        product = lax.dot_general(
            operand, legendre_ref[s], (((1,), (1,)), ((), ())), preferred_element_type=f32
        )
        for x in range(2):
            for y in range(2):
                row = x * 32 + y * 8
                value = product[row : row + 8] * keep + product[row + 16 : row + 24] * flipped
                out_ref[s, 0, 2 * x + y] = value[0:4].astype(bf16)
                out_ref[s, 1, 2 * x + y] = value[4:8].astype(bf16)
        return carry

    lax.fori_loop(0, SLOTS, direct, 0)


def per_device(coeffs, legendre, slot_wave, lon_points, quad_weights):
    waves = jnp.pad(slot_wave.reshape(WAVE, SLOTS).T, ((0, 2), (0, 0)))
    latitudes = jnp.stack(
        [lon_points[:HALF].astype(f32), quad_weights[:HALF], quad_weights[HALF:][::-1]], axis=0
    )
    latitudes = jnp.pad(latitudes, ((0, 5), (0, 0)))
    vmem = pl.BlockSpec(memory_space=pltpu.VMEM)
    smem = pl.BlockSpec(memory_space=pltpu.SMEM)
    scratch = [
        pltpu.VMEM((32, DEGREES), f32),
        pltpu.VMEM((32, DEGREES), bf16),
        pltpu.VMEM((LEV, 32, DEGREES), bf16),
        pltpu.VMEM((SLOTS, 8, DEGREES), f32),
        pltpu.VMEM((DEGREES // LANES, 80, LANES), f32),
        pltpu.VMEM((SLOTS, LATS, 80, LANES), f32),
        pltpu.VMEM((6, LANES, LANES), f32),
        pltpu.VMEM((LATS, 4, HALF, WIDTH), bf16),
        pltpu.VMEM((8, LANES, LANES), f32),
        pltpu.VMEM((8 * LANES, LANES), f32),
        pltpu.VMEM((WAVE, 8, LANES), bf16),
        pltpu.VMEM((WAVE, 8, LANES), bf16),
        pltpu.VMEM((WAVE, 8, LANES), bf16),
        pltpu.VMEM((WAVE, 8, LANES), bf16),
        pltpu.VMEM((2, SLOTS, 32, LANES), f32),
        pltpu.VMEM((LATS, 4, 64, HALF), bf16),
        pltpu.VMEM((4, 64, WIDTH), f32),
        pltpu.VMEM((4, 32, WIDTH), bf16),
        pltpu.VMEM((8, LATS, 24, LANES), f32),
        pltpu.VMEM((SLOTS, LATS, 64, LANES), f32),
    ] + [pltpu.SemaphoreType.DMA(())] * 6
    return pl.pallas_call(
        kernel,
        out_shape=jax.ShapeDtypeStruct(coeffs.shape, bf16),
        in_specs=[smem, smem, smem, vmem, vmem, vmem, vmem],
        out_specs=vmem,
        scratch_shapes=scratch,
        compiler_params=pltpu.CompilerParams(
            collective_id=0, has_side_effects=True, vmem_limit_bytes=48 * 1024 * 1024
        ),
    )(lon_points, slot_wave, quad_weights, waves, latitudes, coeffs, legendre)


def solution(mesh):
    placed = (P("wave", None, None, "lev", None), P("wave", None, None), P(), P(), P())
    return jax.shard_map(
        per_device,
        mesh=mesh,
        in_specs=placed,
        out_specs=P("wave", None, None, "lev", None),
        check_vma=False,
    )
```

time: 656 us -> 72.3 us (0.11); the launches traced: 644 us -> 71.9 us
  other arithmetic: 313 us -> 0.7 us
  local copies, waits for them, and re-layouts: 141 us -> 7.51 us
  Pallas kernels: 0 us -> 63.7 us
  loops' own time: 49.4 us -> 0 us
  blocking collectives: 45.6 us -> 0 us
  matrix products: 40.9 us -> 0 us
  waiting for transfers between devices: 32.1 us -> 0 us
  starting transfers between devices: 21 us -> 0 us
    cos x24 -> x0, other arithmetic: 255 us -> none  [angle_pair(): return (jnp.cos(angles), jnp.sin(angles))]
    pallas_call x0 -> x1, Pallas kernels: none -> 63.7 us  [per_device(): pl.pallas_call(kernel, out_shape=jax.ShapeDtypeStruct(coeffs.shape, bf16)...]
    another operation x3 -> x0, loops' own time: 49.4 us -> none  [the longest x1 33.3 us: per_device(): spectral_rows = lax.map(spectral_group, (forcing, points_all))]
    dot_general x16 -> x0, matrix products: 40.9 us -> none  [the longest x6 19.6 us: to_spectral(): jnp.einsum('lcbq,sq->lbcs', shaped, base_table, precision=highest)]
    dynamic_update_slice x12 -> x0, local copies, waits for them, and re-layouts: 35 us -> none  [per_device(): grid_field = lax.map(grid_group, (grouped, points_all))]
    all_to_all x1 -> x0, blocking collectives: 34 us -> none  [per_device(): lax.all_to_all(weighted, 'wave', split_axis=2, concat_axis=1, tiled=True)]
    all_to_all x1 -> x0, waiting for transfers between devices: 32.1 us -> none  [per_device(): lax.all_to_all(outgoing, 'wave', split_axis=1, concat_axis=2, tiled=True)]
    dynamic_slice x23 -> x0, local copies, waits for them, and re-layouts: 27.4 us -> none  [the longest x6 12.8 us: per_device(): spectral_rows = lax.map(spectral_group, (forcing, points_all))]
  transfers between devices with their start and end apart: 1 -> 0, of which waited for: 1 -> 0; matrix products, arithmetic and copies ran while one was open for 0% -> 0% of each run, Pallas kernels for 0% -> 0%
where the time goes in v1:
time: 72.3 us; the launch traced here: 71.9 us
  Pallas kernels  63.7 us (88%)
  local copies, waits for them, and re-layouts  7.51 us (10%)
    pallas_call x1, Pallas kernels, per_device(): pl.pallas_call(kernel, out_shape=jax.ShapeDtypeStruct(coeffs.shape, bf16)...  63.7 us
    unnamed x11, local copies, waits for them, and re-layouts  5.75 us

profile of v1, /device:TPU:1, one launch (start us, length us, event | category | flops | bytes accessed | tf_op | source)
XLA Modules:
  0.0 71.9 jit_solution(17792631016548673903)
XLA Ops:
  0.0 0.7 slice_convert_fusion
  0.7 0.8 %fusion = (f32[384]{0:T(512)S(1)}, f32[384]{0:T(512)S(1)}) fusion(f32[768]{0:T(1024)} %quad_s.1), kind=kLoop, calls=%fused_computation.4 | loop fusion | bytes 6144 | tf_op jit(solution)/shard_map/slice | solution.py:399
  1.5 0.1 rev.3
  1.6 0.8 %reshape.3 = s32[128,6]{1,0:T(8,128)S(1)} reshape(s32[768]{0:T(1024)} %slot_s.1) | data formatting | bytes 6144 | tf_op jit(solution)/shard_map/reshape | solution.py:397
  2.4 0.1 copy.6
  2.5 0.0 copy-start
  2.5 2.0 %copy-done = bf16[6,768,384]{2,1,0:T(8,128)(2,1)S(1)} copy-done((bf16[6,768,384]{2,1,0:T(8,128)(2,1)S(1)}, bf16[6,768,384]{2,1,0:T(8,128)(2,1)}, u32[]{:S(2)}) %copy-start) | copy-done | bytes 3538968
  4.5 0.0 copy-start.1
  4.5 1.0 %copy-done.1 = bf16[6,2,4,4,768]{4,3,2,1,0:T(4,128)(2,1)S(1)} copy-done((bf16[6,2,4,4,768]{4,3,2,1,0:T(4,128)(2,1)S(1)}, bf16[6,2,4,4,768]{4,3,2,1,0:T(4,128)(2,1)}, u32[]{:S(2)}) %copy-start.1) | copy-done | bytes 294936
  5.5 0.0 copy-start.2
  5.5 0.7 copy-done.2
  6.1 0.0 copy-start.3
  6.1 0.7 copy-done.3
  6.8 0.0 copy-start.4
  6.8 0.7 copy-done.4
  7.5 63.7 %shard_map.55 = bf16[6,2,4,4,768]{4,3,2,1,0:T(4,128)(2,1)S(1)} custom-call(s32[768]{0:T(1024)S(1)} %copy-done.4, s32[768]{0:T(1024)S(1)} %copy-done.2, f32[768]{0:T(1024)S(1)} %copy-done.3, s32[8,128]{1,0:T(8,128)S(1)} %pad.8.waves_ref, f32[8,384]{1,0:T(8,128)S(1)} %select_maximum_fusion.lat_ref, bf16[6,2,4,4,768]{4,3,2,1,0:T(4,128)(2,1)S(1)} %copy-done.1, ...), custom_call_target="tpu_custom_call" | custom-call | tf_op jit(solution)/shard_map/pallas_call | solution.py:426
  71.2 0.7 copy.8
  (5 shorter events, 0.0 us)
Async XLA Ops:
  2.5 2.0 %copy-start = (bf16[6,768,384]{2,1,0:T(8,128)(2,1)S(1)}, bf16[6,768,384]{2,1,0:T(8,128)(2,1)}, u32[]{:S(2)}) copy-start(bf16[6,768,384]{2,1,0:T(8,128)(2,1)} %legendre_ref.1) | copy-start | bytes 10616836
  4.5 1.0 %copy-start.1 = (bf16[6,2,4,4,768]{4,3,2,1,0:T(4,128)(2,1)S(1)}, bf16[6,2,4,4,768]{4,3,2,1,0:T(4,128)(2,1)}, u32[]{:S(2)}) copy-start(bf16[6,2,4,4,768]{4,3,2,1,0:T(4,128)(2,1)} %coeffs_ref.1) | copy-start | bytes 884740
  5.5 0.7 copy-start.2
  6.1 0.7 copy-start.3
  6.8 0.7 copy-start.4

commit v2 on v1

--- a/solution.py
+++ b/solution.py
@@ -42,22 +42,69 @@
 
 
 def kernel(
-    lon_s, slot_s, quad_s, waves_ref, lat_ref, coeffs_ref, legendre_ref, out_ref,
+    lon_h, slot_h, quad_h, coeffs_h, legendre_h, out_ref,
+    lon_s, slot_s, quad_s, lon_v, slot_v, quad_v, coeffs_ref, legendre_ref, waves_ref, lat_ref,
     sums, lev_send, lev_recv, lower, stage, four, column, tables, planes, wide,
     send_one, recv_one, send_two, recv_two, pairs, left, sumpq, leftback, planes_two, weighted,
-    lev_ssem, lev_rsem, ssem_one, rsem_one, ssem_two, rsem_two,
+    mass_sums, mass_send, mass_recv, mass_lower, low_four,
+    small_sem, coeffs_sem, legendre_sem,
+    lev_ssem, lev_rsem, mass_ssem, mass_rsem, ssem_one, rsem_one, ssem_two, rsem_two,
 ):
     me = lax.axis_index("wave")
     lev = lax.axis_index("lev")
     barrier = pltpu.get_barrier_semaphore()
+    small = [
+        pltpu.make_async_copy(src, dst, small_sem.at[i])
+        for i, (src, dst) in enumerate(
+            ((slot_h, slot_s), (lon_h, lon_s), (quad_h, quad_s), (slot_h, slot_v), (lon_h, lon_v), (quad_h, quad_v))
+        )
+    ]
+    load_coeffs = pltpu.make_async_copy(coeffs_h, coeffs_ref, coeffs_sem)
+
+    def load_legendre(s):
+        return pltpu.make_async_copy(legendre_h.at[s], legendre_ref.at[s], legendre_sem.at[s])
+
+    small[0].start()
+    load_coeffs.start()
+    for s in range(SLOTS):
+        load_legendre(s).start()
+    for copy in small[1:]:
+        copy.start()
+    for i in range(1, LEV):
+        pl.semaphore_signal(barrier, inc=1, device_id=(me, lax.rem(lev + i, LEV)), device_id_type=MESH)
 
     def greet(i, carry):
         pl.semaphore_signal(barrier, inc=1, device_id=(lax.rem(me + i, WAVE), lev), device_id_type=MESH)
         return carry
 
     lax.fori_loop(1, WAVE, greet, 0)
-    for i in range(1, LEV):
-        pl.semaphore_signal(barrier, inc=1, device_id=(me, lax.rem(lev + i, LEV)), device_id_type=MESH)
+    small[0].wait()
+    load_coeffs.wait()
+
+    degree = lax.broadcasted_iota(jnp.int32, (1, DEGREES), 1)
+    place = (0, 4, 2, 6)
+
+    def put_rows(start, stride, value):
+        for b in range(DEGREES // LANES):
+            stage[b, pl.ds(start, 4, stride=stride), :] = value[:, b * LANES : (b + 1) * LANES]
+
+    def forward(s, carry):
+        load_legendre(s).wait()
+        m = slot_s[me * SLOTS + s]
+        keep = (degree >= m).astype(f32)
+        flipped = keep * (1.0 - 2.0 * ((degree + m) & 1).astype(f32))
+        for r in range(2):
+            for f in range(4):
+                value = coeffs_ref[s, r, f].astype(f32)
+                put_rows(r * 32 + place[f], 8, value * keep)
+                put_rows(r * 32 + place[f] + 1, 8, value * flipped)
+        operand = jnp.concatenate([stage[b] for b in range(DEGREES // LANES)], axis=1).astype(bf16)
+        product = jnp.dot(operand, legendre_ref[s], preferred_element_type=f32) * ROOT
+        for t in range(LATS):
+            four[s, t] = product[:, t * LANES : (t + 1) * LANES]
+        return carry
+
+    lax.fori_loop(0, SLOTS, forward, 0)
 
     sums[24:32, :] = jnp.zeros((8, DEGREES), f32)
     for s in range(SLOTS):
@@ -66,13 +113,95 @@
                 row = s * 4 + r * 2 + f - 1
                 sums[row : row + 1, :] = jnp.sum(coeffs_ref[s, r, f].astype(f32), axis=0, keepdims=True)
     lev_send[...] = sums[...].astype(bf16)
+
+    def to_levels(outgoing, incoming, ssem, rsem):
+        for i in range(1, LEV):
+            pltpu.make_async_remote_copy(
+                src_ref=outgoing, dst_ref=incoming.at[lev], send_sem=ssem, recv_sem=rsem,
+                device_id=(me, lax.rem(lev + i, LEV)), device_id_type=MESH,
+            ).start()
+
+    def from_levels(outgoing, incoming, ssem, rsem):
+        part = incoming.at[pl.ds(0, LEV - 1)]
+        pltpu.make_async_copy(part, part, rsem).wait()
+        pltpu.make_async_copy(part, part, ssem).wait()
+        total = jnp.zeros(outgoing.shape, f32)
+        for k in range(LEV):
+            total = total + jnp.where(k < lev, incoming[k].astype(f32), 0.0)
+        return total
+
+    def spread(step, carry):
+        planes[step, 104:128, :] = jnp.zeros((24, LANES), f32)
+        for t in range(LATS):
+            for j in range(SLOTS):
+                base = (t * SLOTS + j) * 6
+                planes[step, base : base + 6, :] = four[j, t, pl.ds(pl.multiple_of(step * 8, 8), 8), :][0:6]
+        return carry
+
+    lax.fori_loop(0, 8, spread, 0)
+    for rv in range(8):
+        wide[pl.ds(rv, LANES, stride=8), :] = planes[rv].T
+
+    def narrow_one(i, carry):
+        rows = pl.ds(pl.multiple_of(i * 128, 128), 128)
+        send_one[pl.ds(i * 16, 16)] = wide[rows, :].reshape(16, 8, LANES).astype(bf16)
+        return carry
+
+    lax.fori_loop(0, 8, narrow_one, 0)
+
+    def exchange(outgoing, incoming, ssem, rsem):
+        pltpu.make_async_copy(outgoing.at[me], incoming.at[me], rsem).start()
+
+        def put(peer):
+            pltpu.make_async_remote_copy(
+                src_ref=outgoing.at[peer], dst_ref=incoming.at[me], send_sem=ssem, recv_sem=rsem,
+                device_id=(peer, lev), device_id_type=MESH,
+            ).start()
+
+        put(lax.rem(me + WAVE // 2, WAVE))
+
+        def both(i, carry):
+            put(lax.rem(me + WAVE // 2 - i, WAVE))
+            put(lax.rem(me + WAVE // 2 + i, WAVE))
+            return carry
+
+        lax.fori_loop(1, WAVE // 2, both, 0)
+
+    def settle(outgoing, incoming, ssem, rsem):
+        pltpu.make_async_copy(incoming, incoming, rsem).wait()
+        part = outgoing.at[pl.ds(0, WAVE - 1)]
+        pltpu.make_async_copy(part, part, ssem).wait()
+
     lev_recv[lev] = jnp.zeros((32, DEGREES), bf16)
+    mass_recv[lev] = jnp.zeros((SLOTS, 16, LANES), bf16)
     pl.semaphore_wait(barrier, WAVE - 1 + LEV - 1)
-    for i in range(1, LEV):
-        pltpu.make_async_remote_copy(
-            src_ref=lev_send, dst_ref=lev_recv.at[lev], send_sem=lev_ssem, recv_sem=lev_rsem,
-            device_id=(me, lax.rem(lev + i, LEV)), device_id_type=MESH,
-        ).start()
+    exchange(send_one, recv_one, ssem_one, rsem_one)
+    to_levels(lev_send, lev_recv, lev_ssem, lev_rsem)
+    for copy in small[1:]:
+        copy.wait()
+
+    number = lax.broadcasted_iota(jnp.int32, (8, DEGREES), 1).astype(f32)
+    group = jnp.floor((number + 0.5) * (1.0 / SLOTS))
+    mine = (number - group * SLOTS) == lax.broadcasted_iota(jnp.int32, (8, DEGREES), 0).astype(f32)
+    every = jnp.concatenate([slot_v[pl.ds(b * LANES, LANES)].reshape(1, LANES) for b in range(6)], axis=1)
+    high = jnp.where(mine, (every >> 4).astype(f32), 0.0)
+    low = jnp.where(mine, (every & 15).astype(f32), 0.0)
+    ahead = lax.broadcasted_iota(jnp.int32, (DEGREES, LANES), 0) - SLOTS * lax.broadcasted_iota(
+        jnp.int32, (DEGREES, LANES), 1
+    )
+    belongs = jnp.where((ahead >= 0) & (ahead < SLOTS), 1.0, 0.0).astype(bf16)
+    split = jnp.dot(
+        jnp.concatenate([high, low], axis=0).astype(bf16), belongs, preferred_element_type=f32
+    )
+    waves_ref[...] = (split[0:8] * 16.0 + split[8:16]).astype(jnp.int32)
+    flip = lax.broadcasted_iota(jnp.int32, (LANES, LANES), 0) + lax.broadcasted_iota(jnp.int32, (LANES, LANES), 1)
+    flip = jnp.where(flip == LANES - 1, 1.0, 0.0)
+    for t in range(LATS):
+        south = jnp.broadcast_to(quad_v[pl.ds((5 - t) * LANES, LANES)].reshape(1, LANES), (8, LANES))
+        south = jnp.dot(south, flip, preferred_element_type=f32, precision=lax.Precision.HIGHEST)
+        lat_ref[t, 0:1, :] = lon_v[pl.ds(t * LANES, LANES)].reshape(1, LANES).astype(f32)
+        lat_ref[t, 1:2, :] = quad_v[pl.ds(t * LANES, LANES)].reshape(1, LANES)
+        lat_ref[t, 2:3, :] = south[0:1]
 
     for q in range(3):
         first = waves_ref[2 * q : 2 * q + 1, :]
@@ -102,131 +231,7 @@
             tables[t, 2 * parity + 1, rows, columns] = (horner(SINE, y) * x).astype(bf16)
         return carry
 
-    lax.fori_loop(0, LATS * 6, table_block, 0)
-
-    everyone = pltpu.make_async_copy(lev_recv.at[pl.ds(0, LEV - 1)], lev_recv.at[pl.ds(0, LEV - 1)], lev_rsem)
-    everyone.wait()
-    pltpu.make_async_copy(lev_recv.at[pl.ds(0, LEV - 1)], lev_recv.at[pl.ds(0, LEV - 1)], lev_ssem).wait()
-    total = jnp.zeros((32, DEGREES), f32)
-    for k in range(LEV):
-        total = total + jnp.where(k < lev, lev_recv[k].astype(f32), 0.0)
-    sums[...] = total
-    for s in range(SLOTS):
-        lower[s, 0:4, :] = sums[s * 4 : s * 4 + 4, :]
-
-    degree = lax.broadcasted_iota(jnp.int32, (1, DEGREES), 1)
-    place = (0, 4, 2, 6)
-    for b in range(DEGREES // LANES):
-        stage[b, 72:80, :] = jnp.zeros((8, LANES), f32)
-
-    def put_rows(start, stride, value):
-        for b in range(DEGREES // LANES):
-            stage[b, pl.ds(start, 4, stride=stride), :] = value[:, b * LANES : (b + 1) * LANES]
-
-    def forward(s, carry):
-        m = slot_s[me * SLOTS + s]
-        keep = (degree >= m).astype(f32)
-        flipped = keep * (1.0 - 2.0 * ((degree + m) & 1).astype(f32))
-        for r in range(2):
-            for f in range(4):
-                value = coeffs_ref[s, r, f].astype(f32)
-                put_rows(r * 32 + place[f], 8, value * keep)
-                put_rows(r * 32 + place[f] + 1, 8, value * flipped)
-        extra = lower[s, 0:4, :]
-        put_rows(64, 2, extra * keep)
-        put_rows(65, 2, extra * flipped)
-        operand = jnp.concatenate([stage[b] for b in range(DEGREES // LANES)], axis=1).astype(bf16)
-        product = jnp.dot(operand, legendre_ref[s], preferred_element_type=f32) * ROOT
-        for t in range(LATS):
-            four[s, t] = product[:, t * LANES : (t + 1) * LANES]
-        return carry
-
-    lax.fori_loop(0, SLOTS, forward, 0)
-
-    def spread(step, carry):
-        r = step // 4
-        v = lax.rem(step, 4)
-        for t in range(LATS):
-            for j in range(SLOTS):
-                base = (t * SLOTS + j) * 7
-                planes[step, base : base + 7, :] = four[j, t, pl.ds(pl.multiple_of(step * 8, 8), 8), :][0:7]
-        planes[step, 126:128, :] = jnp.zeros((2, LANES), f32)
-        return carry
-
-    lax.fori_loop(0, 8, spread, 0)
-    for r in range(2):
-        for ns in range(2):
-            for t in range(LATS):
-                for j in range(SLOTS):
-                    base = (t * SLOTS + j) * 7 + 6
-                    row = 64 + r * 4 + ns
-                    planes[r * 4 + ns, base : base + 1, :] = four[j, t, row : row + 1, :]
-    for rv in range(8):
-        wide[pl.ds(rv, LANES, stride=8), :] = planes[rv].T
-
-    def narrow_one(i, carry):
-        rows = pl.ds(pl.multiple_of(i * 128, 128), 128)
-        send_one[pl.ds(i * 16, 16)] = wide[rows, :].reshape(16, 8, LANES).astype(bf16)
-        return carry
-
-    lax.fori_loop(0, 8, narrow_one, 0)
-
-    def exchange(outgoing, incoming, ssem, rsem):
-        pltpu.make_async_copy(outgoing.at[me], incoming.at[me], rsem).start()
-
-        def put(peer):
-            pltpu.make_async_remote_copy(
-                src_ref=outgoing.at[peer], dst_ref=incoming.at[me], send_sem=ssem, recv_sem=rsem,
-                device_id=(peer, lev), device_id_type=MESH,
-            ).start()
-
-        put(lax.rem(me + WAVE // 2, WAVE))
-
-        def both(i, carry):
-            put(lax.rem(me + WAVE // 2 - i, WAVE))
-            put(lax.rem(me + WAVE // 2 + i, WAVE))
-            return carry
-
-        lax.fori_loop(1, WAVE // 2, both, 0)
-
-    def settle(outgoing, incoming, ssem, rsem):
-        pltpu.make_async_copy(incoming, incoming, rsem).wait()
-        part = outgoing.at[pl.ds(0, WAVE - 1)]
-        pltpu.make_async_copy(part, part, ssem).wait()
-
-    exchange(send_one, recv_one, ssem_one, rsem_one)
-
-    def level_sum(value, first, second):
-        row = lax.broadcasted_iota(jnp.int32, value.shape, 0)
-        level = row & 3
-        value = value + jnp.where(level >= 1, pltpu.roll(value, 1, 0), 0.0)
-        value = value + jnp.where(level >= 2, pltpu.roll(value, 2, 0), 0.0)
-        return (value + jnp.where(row < 4, first, second)) * 0.25
-
-    def local(s, carry):
-        m = slot_s[me * SLOTS + s]
-        row = lax.broadcasted_iota(jnp.int32, (8, LANES), 0)
-        live = jnp.where((row < 4) | (m > 0), 1.0, 0.0)
-        for t in range(LATS):
-            columns = slice(t * LANES, (t + 1) * LANES)
-            inside = (2.0 * m.astype(f32) < lat_ref[0:1, columns]).astype(f32)
-            for ns in range(2):
-                factor = live * (inside * lat_ref[1 + ns : 2 + ns, columns])
-
-                def rows(place, low):
-                    return level_sum(
-                        four[s, t, pl.ds(place + ns, 8, stride=8), :],
-                        four[s, t, low + ns : low + ns + 1, :],
-                        four[s, t, low + ns + 4 : low + ns + 5, :],
-                    )
-
-                weighted[s, t, ns * 16 + 8 : ns * 16 + 16, :] = rows(2, 66) * factor
-                weighted[s, t, 32 + ns * 16 + 8 : 32 + ns * 16 + 16, :] = (
-                    four[s, t, pl.ds(6 + ns, 8, stride=8), :] + rows(4, 64)
-                ) * factor
-        return carry
-
-    lax.fori_loop(0, SLOTS, local, 0)
+    lax.fori_loop(0, 2 * 6, table_block, 0)
 
     settle(send_one, recv_one, ssem_one, rsem_one)
 
@@ -242,21 +247,39 @@
 
     widen(recv_one)
 
+    mass_sums[...] = jnp.zeros((SLOTS, 16, LANES), f32)
+    for t in range(LATS):
+        for j in range(SLOTS):
+            base = (t * SLOTS + j) * 6 + 4
+            for r in range(2):
+                value = planes[r * 4, base : base + 2, :]
+                for v in range(1, 4):
+                    value = value + planes[r * 4 + v, base : base + 2, :]
+                row = r * 6 + t * 2
+                mass_sums[j, row : row + 2, :] = value
+    mass_send[...] = mass_sums[...].astype(bf16)
+    to_levels(mass_send, mass_recv, mass_ssem, mass_rsem)
+    lax.fori_loop(2 * 6, LATS * 6, table_block, 0)
+
+    for t in range(LATS):
+        for r in range(2):
+            for j in range(SLOTS):
+                base = (t * SLOTS + j) * 6
+                for v in range(4):
+                    rv = r * 4 + v
+                    pairs[t, r, j, v * 4 : v * 4 + 4, :] = planes[rv, base : base + 4, :]
+                    pairs[t, r, j, 16 + v * 4 : 18 + v * 4, :] = planes[rv, base + 4 : base + 6, :]
+    mass_lower[...] = from_levels(mass_send, mass_recv, mass_ssem, mass_rsem)
     for t in range(LATS):
         points = jnp.full((1, LANES), lon_s[me + LANES * t], jnp.int32)
         for r in range(2):
             for j in range(SLOTS):
-                base = (t * SLOTS + j) * 7
+                base = (t * SLOTS + j) * 6 + 4
+                row = r * 6 + t * 2
+                run = mass_lower[j, row : row + 2, :]
                 for v in range(4):
-                    rv = r * 4 + v
-                    pairs[r, j, v * 4 : v * 4 + 4, :] = planes[rv, base : base + 4, :]
-                    pairs[r, j, 16 + v * 4 : 18 + v * 4, :] = planes[rv, base + 4 : base + 6, :]
-                for ns in range(2):
-                    run = planes[r * 4 + ns, base + 6 : base + 7, :]
-                    for v in range(4):
-                        run = run + planes[r * 4 + v, base + 4 + ns : base + 5 + ns, :]
-                        row = 18 + v * 4 + ns
-                        pairs[r, j, row : row + 1, :] = run * 0.25
+                    run = run + planes[r * 4 + v, base : base + 2, :]
+                    pairs[t, r, j, 18 + v * 4 : 20 + v * 4, :] = run * 0.25
         for q in range(3):
             first = waves_ref[2 * q : 2 * q + 1, :]
             second = waves_ref[2 * q + 1 : 2 * q + 2, :]
@@ -269,10 +292,10 @@
             odd_factor = jnp.where(2 * odd < points, 2.0, 0.0)
             pick = jnp.broadcast_to(even_first.astype(f32), (32, LANES)) > 0.5
             columns = slice(q * LANES, (q + 1) * LANES)
-            real_even = jnp.where(pick, pairs[0, 2 * q], pairs[0, 2 * q + 1]) * even_factor
-            real_odd = jnp.where(pick, pairs[0, 2 * q + 1], pairs[0, 2 * q]) * odd_factor
-            imag_even = jnp.where(pick, pairs[1, 2 * q], pairs[1, 2 * q + 1]) * even_factor
-            imag_odd = jnp.where(pick, pairs[1, 2 * q + 1], pairs[1, 2 * q]) * odd_factor
+            real_even = jnp.where(pick, pairs[t, 0, 2 * q], pairs[t, 0, 2 * q + 1]) * even_factor
+            real_odd = jnp.where(pick, pairs[t, 0, 2 * q + 1], pairs[t, 0, 2 * q]) * odd_factor
+            imag_even = jnp.where(pick, pairs[t, 1, 2 * q], pairs[t, 1, 2 * q + 1]) * even_factor
+            imag_odd = jnp.where(pick, pairs[t, 1, 2 * q + 1], pairs[t, 1, 2 * q]) * odd_factor
             left[t, 0, 0:32, columns] = real_even.astype(bf16)
             left[t, 0, 32:64, columns] = (sigma * real_even).astype(bf16)
             left[t, 1, 0:32, columns] = imag_even.astype(bf16)
@@ -366,6 +389,50 @@
 
     lax.fori_loop(0, 8, narrow_two, 0)
     exchange(send_two, recv_two, ssem_two, rsem_two)
+    def level_sum(value, first, second):
+        row = lax.broadcasted_iota(jnp.int32, value.shape, 0)
+        level = row & 3
+        value = value + jnp.where(level >= 1, pltpu.roll(value, 1, 0), 0.0)
+        value = value + jnp.where(level >= 2, pltpu.roll(value, 2, 0), 0.0)
+        return (value + jnp.where(row < 4, first, second)) * 0.25
+
+    def local(s, carry):
+        m = slot_s[me * SLOTS + s]
+        keep = (degree >= m).astype(f32)
+        flipped = keep * (1.0 - 2.0 * ((degree + m) & 1).astype(f32))
+        side = lax.broadcasted_iota(jnp.int32, (8, DEGREES), 0)
+        extra = lower[s] * jnp.where(side < 4, keep, flipped)
+        extra = jnp.concatenate([extra, jnp.zeros((8, DEGREES), f32)], axis=0).astype(bf16)
+        product = jnp.dot(extra, legendre_ref[s], preferred_element_type=f32) * ROOT
+        for t in range(LATS):
+            low_four[t] = product[0:8, t * LANES : (t + 1) * LANES]
+        row = lax.broadcasted_iota(jnp.int32, (8, LANES), 0)
+        live = jnp.where((row < 4) | (m > 0), 1.0, 0.0)
+        for t in range(LATS):
+            inside = (2.0 * m.astype(f32) < lat_ref[t, 0:1, :]).astype(f32)
+            for ns in range(2):
+                factor = live * (inside * lat_ref[t, 1 + ns : 2 + ns, :])
+
+                def rows(place, low):
+                    return level_sum(
+                        four[s, t, pl.ds(place + ns, 8, stride=8), :],
+                        low_four[t, 4 * ns + low : 4 * ns + low + 1, :],
+                        low_four[t, 4 * ns + low + 2 : 4 * ns + low + 3, :],
+                    )
+
+                weighted[s, t, ns * 16 + 8 : ns * 16 + 16, :] = rows(2, 1) * factor
+                weighted[s, t, 32 + ns * 16 + 8 : 32 + ns * 16 + 16, :] = (
+                    four[s, t, pl.ds(6 + ns, 8, stride=8), :] + rows(4, 0)
+                ) * factor
+        return carry
+
+    total = from_levels(lev_send, lev_recv, lev_ssem, lev_rsem)
+    sums[...] = total
+    for s in range(SLOTS):
+        lower[s, 0:4, :] = sums[s * 4 : s * 4 + 4, :]
+        lower[s, 4:8, :] = sums[s * 4 : s * 4 + 4, :]
+    lax.fori_loop(0, SLOTS, local, 0)
+
     settle(send_two, recv_two, ssem_two, rsem_two)
     widen(recv_two)
     for rv in range(8):
@@ -394,20 +461,25 @@
 
 
 def per_device(coeffs, legendre, slot_wave, lon_points, quad_weights):
-    waves = jnp.pad(slot_wave.reshape(WAVE, SLOTS).T, ((0, 2), (0, 0)))
-    latitudes = jnp.stack(
-        [lon_points[:HALF].astype(f32), quad_weights[:HALF], quad_weights[HALF:][::-1]], axis=0
-    )
-    latitudes = jnp.pad(latitudes, ((0, 5), (0, 0)))
     vmem = pl.BlockSpec(memory_space=pltpu.VMEM)
-    smem = pl.BlockSpec(memory_space=pltpu.SMEM)
+    outside = pl.BlockSpec(memory_space=pltpu.HBM)
     scratch = [
+        pltpu.SMEM((DEGREES,), jnp.int32),
+        pltpu.SMEM((DEGREES,), jnp.int32),
+        pltpu.SMEM((DEGREES,), f32),
+        pltpu.VMEM((DEGREES,), jnp.int32),
+        pltpu.VMEM((DEGREES,), jnp.int32),
+        pltpu.VMEM((DEGREES,), f32),
+        pltpu.VMEM(coeffs.shape, bf16),
+        pltpu.VMEM(legendre.shape, bf16),
+        pltpu.VMEM((8, LANES), jnp.int32),
+        pltpu.VMEM((LATS, 8, LANES), f32),
         pltpu.VMEM((32, DEGREES), f32),
         pltpu.VMEM((32, DEGREES), bf16),
         pltpu.VMEM((LEV, 32, DEGREES), bf16),
         pltpu.VMEM((SLOTS, 8, DEGREES), f32),
-        pltpu.VMEM((DEGREES // LANES, 80, LANES), f32),
-        pltpu.VMEM((SLOTS, LATS, 80, LANES), f32),
+        pltpu.VMEM((DEGREES // LANES, 64, LANES), f32),
+        pltpu.VMEM((SLOTS, LATS, 64, LANES), f32),
         pltpu.VMEM((6, LANES, LANES), f32),
         pltpu.VMEM((LATS, 4, HALF, WIDTH), bf16),
         pltpu.VMEM((8, LANES, LANES), f32),
@@ -416,23 +488,31 @@
         pltpu.VMEM((WAVE, 8, LANES), bf16),
         pltpu.VMEM((WAVE, 8, LANES), bf16),
         pltpu.VMEM((WAVE, 8, LANES), bf16),
-        pltpu.VMEM((2, SLOTS, 32, LANES), f32),
+        pltpu.VMEM((LATS, 2, SLOTS, 32, LANES), f32),
         pltpu.VMEM((LATS, 4, 64, HALF), bf16),
         pltpu.VMEM((4, 64, WIDTH), f32),
         pltpu.VMEM((4, 32, WIDTH), bf16),
         pltpu.VMEM((8, LATS, 24, LANES), f32),
         pltpu.VMEM((SLOTS, LATS, 64, LANES), f32),
-    ] + [pltpu.SemaphoreType.DMA(())] * 6
+        pltpu.VMEM((SLOTS, 16, LANES), f32),
+        pltpu.VMEM((SLOTS, 16, LANES), bf16),
+        pltpu.VMEM((LEV, SLOTS, 16, LANES), bf16),
+        pltpu.VMEM((SLOTS, 16, LANES), f32),
+        pltpu.VMEM((LATS, 8, LANES), f32),
+        pltpu.SemaphoreType.DMA((6,)),
+        pltpu.SemaphoreType.DMA(()),
+        pltpu.SemaphoreType.DMA((SLOTS,)),
+    ] + [pltpu.SemaphoreType.DMA(())] * 8
     return pl.pallas_call(
         kernel,
         out_shape=jax.ShapeDtypeStruct(coeffs.shape, bf16),
-        in_specs=[smem, smem, smem, vmem, vmem, vmem, vmem],
+        in_specs=[outside] * 5,
         out_specs=vmem,
         scratch_shapes=scratch,
         compiler_params=pltpu.CompilerParams(
-            collective_id=0, has_side_effects=True, vmem_limit_bytes=48 * 1024 * 1024
+            collective_id=0, has_side_effects=True, vmem_limit_bytes=63 * 1024 * 1024
         ),
-    )(lon_points, slot_wave, quad_weights, waves, latitudes, coeffs, legendre)
+    )(lon_points, slot_wave, quad_weights, coeffs, legendre)
 
 
 def solution(mesh):

time: 72.3 us -> 62.2 us (0.86)
  local copies, waits for them, and re-layouts: 7.51 us -> 1.78 us
  Pallas kernels: 63.7 us -> 60.3 us
    unnamed x11 -> x1, local copies, waits for them, and re-layouts: 5.75 us -> 1.78 us
    pallas_call x1, Pallas kernels: 63.7 us -> 60.3 us  [per_device(): pl.pallas_call(kernel, out_shape=jax.ShapeDtypeStruct(coeffs.shape, bf16)...]
    reshape x2 -> x0, local copies, waits for them, and re-layouts: 0.88 us -> none  [per_device(): waves = jnp.pad(slot_wave.reshape(WAVE, SLOTS).T, ((0, 2), (0, 0)))]
    slice x1 -> x0, local copies, waits for them, and re-layouts: 0.76 us -> none  [per_device(): quad_weights[:HALF]]
where the time goes in v2:
time: 62.2 us; the launch traced here: 62.1 us
  Pallas kernels  60.3 us (97%)
  local copies, waits for them, and re-layouts  1.78 us (3%)
    pallas_call x1, Pallas kernels, per_device(): pl.pallas_call(kernel, out_shape=jax.ShapeDtypeStruct(coeffs.shape, bf16)...  60.3 us
    unnamed x1, local copies, waits for them, and re-layouts  1.78 us

profile of v2, /device:TPU:1, one launch (start us, length us, event | category | flops | bytes accessed | tf_op | source)
XLA Modules:
  0.0 62.1 jit_solution(7279128480417331439)
XLA Ops:
  0.0 60.3 %shard_map.55 = bf16[6,2,4,4,768]{4,3,2,1,0:T(4,128)(2,1)} custom-call(s32[768]{0:T(1024)} %lon_h.1, s32[768]{0:T(1024)} %slot_h.1, f32[768]{0:T(1024)} %quad_h.1, bf16[6,2,4,4,768]{4,3,2,1,0:T(4,128)(2,1)} %coeffs_h.1, bf16[6,768,384]{2,1,0:T(8,128)(2,1)} %legendre_h.1), custom_call_target="tpu_custom_call" | custom-call | tf_op jit(solution)/shard_map/pallas_call | solution.py:506
  60.3 1.8 %copy.7 = bf16[6,2,4,4,768]{4,3,2,1,0:T(4,128)(2,1)} copy(bf16[6,2,4,4,768]{4,3,2,1,0:T(4,128)(2,1)} %shard_map.55) | data formatting | bytes 589824

commit v3 on v2

--- a/solution.py
+++ b/solution.py
@@ -179,6 +179,8 @@
     to_levels(lev_send, lev_recv, lev_ssem, lev_rsem)
     for copy in small[1:]:
         copy.wait()
+
+    planes_two[:, :, 96:LANES, :] = jnp.zeros((LATS, 2, LANES - 96, LANES), f32)
 
     number = lax.broadcasted_iota(jnp.int32, (8, DEGREES), 1).astype(f32)
     group = jnp.floor((number + 0.5) * (1.0 / SLOTS))
@@ -371,23 +373,22 @@
             imag_odd = (sumpq[3, 0:16, columns] + tau * sumpq[2, 16:32, columns]) * -odd_weight
             for r, one, two in ((0, real_even, real_odd), (1, imag_even, imag_odd)):
                 for j, value in ((2 * q, jnp.where(pick, one, two)), (2 * q + 1, jnp.where(pick, two, one))):
-                    for v in range(4):
-                        planes_two[r * 4 + v, t, j * 4 : j * 4 + 4, :] = value[v * 4 : v * 4 + 4]
+                    planes_two[t, r, j * 16 : j * 16 + 16, :] = value
         return carry
 
     lax.fori_loop(0, LATS, latitude, 0)
 
-    for rv in range(8):
-        filled = planes_two[rv].reshape(LATS * 24, LANES)
-        square = jnp.concatenate([filled, jnp.zeros((LANES - LATS * 24, LANES), f32)], axis=0)
-        wide[pl.ds(rv, LANES, stride=8), :] = square.T
+    for t in range(LATS):
+        for r in range(2):
+            wide[pl.ds(t * 256 + r, LANES, stride=2), :] = planes_two[t, r].T
 
     def narrow_two(i, carry):
-        rows = pl.ds(pl.multiple_of(i * 128, 128), 128)
-        send_two[pl.ds(i * 16, 16)] = wide[rows, :].reshape(16, 8, LANES).astype(bf16)
-        return carry
-
-    lax.fori_loop(0, 8, narrow_two, 0)
+        for t in range(LATS):
+            value = wide[pl.ds(pl.multiple_of(t * 256 + i * 16, 16), 16), :]
+            send_two[pl.ds(i * 8, 8), :, t * LANES : (t + 1) * LANES] = value.reshape(8, 2, LANES).astype(bf16)
+        return carry
+
+    lax.fori_loop(0, 16, narrow_two, 0)
     exchange(send_two, recv_two, ssem_two, rsem_two)
     def level_sum(value, first, second):
         row = lax.broadcasted_iota(jnp.int32, value.shape, 0)
@@ -434,12 +435,21 @@
     lax.fori_loop(0, SLOTS, local, 0)
 
     settle(send_two, recv_two, ssem_two, rsem_two)
-    widen(recv_two)
-    for rv in range(8):
+
+    def widen_two(i, carry):
         for t in range(LATS):
+            value = recv_two[pl.ds(i * 8, 8), :, t * LANES : (t + 1) * LANES].astype(f32)
+            wide[pl.ds(pl.multiple_of(t * 256 + i * 16, 16), 16), :] = value.reshape(16, LANES)
+        return carry
+
+    lax.fori_loop(0, 16, widen_two, 0)
+    for t in range(LATS):
+        for r in range(2):
+            planes[r] = wide[pl.ds(t * 256 + r, LANES, stride=2), :].T
             for j in range(SLOTS):
-                base = (t * SLOTS + j) * 4
-                weighted[j, t, pl.ds(rv, 4, stride=16), :] = planes[rv, base : base + 4, :]
+                for v in range(4):
+                    row = j * 16 + v * 4
+                    weighted[j, t, pl.ds(r * 4 + v, 4, stride=16), :] = planes[r, row : row + 4, :]
 
     def direct(s, carry):
         m = slot_s[me * SLOTS + s]
@@ -486,13 +496,13 @@
         pltpu.VMEM((8 * LANES, LANES), f32),
         pltpu.VMEM((WAVE, 8, LANES), bf16),
         pltpu.VMEM((WAVE, 8, LANES), bf16),
-        pltpu.VMEM((WAVE, 8, LANES), bf16),
-        pltpu.VMEM((WAVE, 8, LANES), bf16),
+        pltpu.VMEM((WAVE, 2, HALF), bf16),
+        pltpu.VMEM((WAVE, 2, HALF), bf16),
         pltpu.VMEM((LATS, 2, SLOTS, 32, LANES), f32),
         pltpu.VMEM((LATS, 4, 64, HALF), bf16),
         pltpu.VMEM((4, 64, WIDTH), f32),
         pltpu.VMEM((4, 32, WIDTH), bf16),
-        pltpu.VMEM((8, LATS, 24, LANES), f32),
+        pltpu.VMEM((LATS, 2, LANES, LANES), f32),
         pltpu.VMEM((SLOTS, LATS, 64, LANES), f32),
         pltpu.VMEM((SLOTS, 16, LANES), f32),
         pltpu.VMEM((SLOTS, 16, LANES), bf16),

time: 62.2 us -> 59.7 us (0.960)
  Pallas kernels: 60.3 us -> 57.8 us
    pallas_call x1, Pallas kernels: 60.3 us -> 57.8 us  [per_device(): pl.pallas_call(kernel, out_shape=jax.ShapeDtypeStruct(coeffs.shape, bf16)...]
where the time goes in v3:
time: 59.7 us; the launch traced here: 59.6 us
  Pallas kernels  57.8 us (97%)
  local copies, waits for them, and re-layouts  1.78 us (3%)
    pallas_call x1, Pallas kernels, per_device(): pl.pallas_call(kernel, out_shape=jax.ShapeDtypeStruct(coeffs.shape, bf16)...  57.8 us
    unnamed x1, local copies, waits for them, and re-layouts  1.78 us

profile of v3, /device:TPU:1, one launch (start us, length us, event | category | flops | bytes accessed | tf_op | source)
XLA Modules:
  0.0 59.6 jit_solution(10842340375104855754)
XLA Ops:
  0.0 57.8 %shard_map.55 = bf16[6,2,4,4,768]{4,3,2,1,0:T(4,128)(2,1)} custom-call(s32[768]{0:T(1024)} %lon_h.1, s32[768]{0:T(1024)} %slot_h.1, f32[768]{0:T(1024)} %quad_h.1, bf16[6,2,4,4,768]{4,3,2,1,0:T(4,128)(2,1)} %coeffs_h.1, bf16[6,768,384]{2,1,0:T(8,128)(2,1)} %legendre_h.1), custom_call_target="tpu_custom_call" | custom-call | tf_op jit(solution)/shard_map/pallas_call | solution.py:516
  57.8 1.8 %copy.7 = bf16[6,2,4,4,768]{4,3,2,1,0:T(4,128)(2,1)} copy(bf16[6,2,4,4,768]{4,3,2,1,0:T(4,128)(2,1)} %shard_map.55) | data formatting | bytes 589824

commit v4 on v3

--- a/solution.py
+++ b/solution.py
@@ -47,7 +47,7 @@
     sums, lev_send, lev_recv, lower, stage, four, column, tables, planes, wide,
     send_one, recv_one, send_two, recv_two, pairs, left, sumpq, leftback, planes_two, weighted,
     mass_sums, mass_send, mass_recv, mass_lower, low_four,
-    small_sem, coeffs_sem, legendre_sem,
+    result, small_sem, coeffs_sem, legendre_sem, store_sem,
     lev_ssem, lev_rsem, mass_ssem, mass_rsem, ssem_one, rsem_one, ssem_two, rsem_two,
 ):
     me = lax.axis_index("wave")
@@ -451,6 +451,9 @@
                     row = j * 16 + v * 4
                     weighted[j, t, pl.ds(r * 4 + v, 4, stride=16), :] = planes[r, row : row + 4, :]
 
+    def store(s):
+        return pltpu.make_async_copy(result.at[s], out_ref.at[s], store_sem.at[s])
+
     def direct(s, carry):
         m = slot_s[me * SLOTS + s]
         keep = (degree >= m).astype(f32) * ROOT
@@ -463,15 +466,17 @@
             for y in range(2):
                 row = x * 32 + y * 8
                 value = product[row : row + 8] * keep + product[row + 16 : row + 24] * flipped
-                out_ref[s, 0, 2 * x + y] = value[0:4].astype(bf16)
-                out_ref[s, 1, 2 * x + y] = value[4:8].astype(bf16)
+                result[s, 0, 2 * x + y] = value[0:4].astype(bf16)
+                result[s, 1, 2 * x + y] = value[4:8].astype(bf16)
+        store(s).start()
         return carry
 
     lax.fori_loop(0, SLOTS, direct, 0)
+    for s in range(SLOTS):
+        store(s).wait()
 
 
 def per_device(coeffs, legendre, slot_wave, lon_points, quad_weights):
-    vmem = pl.BlockSpec(memory_space=pltpu.VMEM)
     outside = pl.BlockSpec(memory_space=pltpu.HBM)
     scratch = [
         pltpu.SMEM((DEGREES,), jnp.int32),
@@ -509,15 +514,17 @@
         pltpu.VMEM((LEV, SLOTS, 16, LANES), bf16),
         pltpu.VMEM((SLOTS, 16, LANES), f32),
         pltpu.VMEM((LATS, 8, LANES), f32),
+        pltpu.VMEM(coeffs.shape, bf16),
         pltpu.SemaphoreType.DMA((6,)),
         pltpu.SemaphoreType.DMA(()),
+        pltpu.SemaphoreType.DMA((SLOTS,)),
         pltpu.SemaphoreType.DMA((SLOTS,)),
     ] + [pltpu.SemaphoreType.DMA(())] * 8
     return pl.pallas_call(
         kernel,
         out_shape=jax.ShapeDtypeStruct(coeffs.shape, bf16),
         in_specs=[outside] * 5,
-        out_specs=vmem,
+        out_specs=outside,
         scratch_shapes=scratch,
         compiler_params=pltpu.CompilerParams(
             collective_id=0, has_side_effects=True, vmem_limit_bytes=63 * 1024 * 1024

time: 59.7 us -> 59.7 us (level)
  no operation moved by 1% of the time
where the time goes in v4:
time: 59.7 us; the launch traced here: 59.5 us
  Pallas kernels  57.7 us (97%)
  local copies, waits for them, and re-layouts  1.78 us (3%)
    pallas_call x1, Pallas kernels, per_device(): pl.pallas_call(kernel, out_shape=jax.ShapeDtypeStruct(coeffs.shape, bf16)...  57.7 us
    unnamed x1, local copies, waits for them, and re-layouts  1.78 us

profile of v4, /device:TPU:1, one launch (start us, length us, event | category | flops | bytes accessed | tf_op | source)
XLA Modules:
  0.0 59.5 jit_solution(14631110243954496878)
XLA Ops:
  0.0 57.7 %shard_map.55 = bf16[6,2,4,4,768]{4,3,2,1,0:T(4,128)(2,1)} custom-call(s32[768]{0:T(1024)} %lon_h.1, s32[768]{0:T(1024)} %slot_h.1, f32[768]{0:T(1024)} %quad_h.1, bf16[6,2,4,4,768]{4,3,2,1,0:T(4,128)(2,1)} %coeffs_h.1, bf16[6,768,384]{2,1,0:T(8,128)(2,1)} %legendre_h.1), custom_call_target="tpu_custom_call" | custom-call | tf_op jit(solution)/shard_map/pallas_call | solution.py:523
  57.8 1.8 %copy.7 = bf16[6,2,4,4,768]{4,3,2,1,0:T(4,128)(2,1)} copy(bf16[6,2,4,4,768]{4,3,2,1,0:T(4,128)(2,1)} %shard_map.55) | data formatting | bytes 589824
